TPU v7x, 32 devices: a whole 2x2x4 slice. The times are simulated.
32 devices in a mesh: groups: 2 (over x), hid: 8 (over z, y), wid: 2 (over core).
Axes of the slice: x: 2, y: 2, z: 4, core: 2. Of those that a mesh axis runs over, the one named last changes fastest.
Arguments:
- act_rows: bfloat16 [128, 8192], P(('groups', 'hid'), 'wid'), parts along dimension 0, may hold values from -6 to 6
- gate_up_mask: int32 [128, 224], P(('groups', 'wid'), 'hid'), parts along dimension 0, may hold values from 0 to 1, as said below
- gate_blocks: bfloat16 [65536, 1024], P(('groups', 'wid'), 'hid'), parts along dimension 0, may hold values from -0.09375 to 0.09375
- up_blocks: bfloat16 [65536, 1024], P(('groups', 'wid'), 'hid'), parts along dimension 0, may hold values from -0.09375 to 0.09375
- down_mask: int32 [448, 64], P(('groups', 'hid'), 'wid'), parts along dimension 0, may hold values from 0 to 1, as said below
- down_blocks: bfloat16 [262144, 256], P(('groups', 'hid'), 'wid'), parts along dimension 0, may hold values from -0.046875 to 0.046875
Outputs:
- layer_out: bfloat16 [128, 8192], P(('groups', 'hid'), 'wid'), parts along dimension 0
There are 2 independent parts, one for each index of `groups`. A program takes and returns all parts, laid end to end along the dimension named above; each array names one. Nothing has to cross between parts.
Inputs may be any that keep to these rules, and one draw needn't show every extreme that they name: `gate_up_mask`: each device tile of the mask (32 by 28 entries) holds at most 128 set entries, and some tile holds exactly 128. `down_mask`: each device tile of the mask (28 by 32 entries) holds at most 128 set entries, and some tile holds exactly 128.
All inputs are finite; a program needn't handle non-finite values.
Results may differ from a plain program's by a relative error of at most 0.005.
Values may be sent and summed in bfloat16 or wider, within the bound.
A program may use at most 128 MiB of HBM per device.

v0:
```python
import jax
import jax.numpy as jnp
from jax import lax
from jax.sharding import PartitionSpec as P


def slot_tables(mask_tile, capacity):
    tile_rows, tile_cols = mask_tile.shape
    flattened = mask_tile.reshape(-1)
    slot_index = jnp.cumsum(flattened) - 1
    occupied = (slot_index[:, None] == jnp.arange(capacity, dtype=jnp.int32)[None, :]) & (
        flattened[:, None] == 1
    )
    occupied = occupied.astype(jnp.float32)
    cell_index = jnp.arange(tile_rows * tile_cols, dtype=jnp.int32)
    row_hot = (
        cell_index[:, None] // tile_cols == jnp.arange(tile_rows, dtype=jnp.int32)[None, :]
    ).astype(jnp.float32)
    col_hot = (
        cell_index[:, None] % tile_cols == jnp.arange(tile_cols, dtype=jnp.int32)[None, :]
    ).astype(jnp.float32)
    pick_rows = jnp.dot(occupied.T, row_hot)
    pick_cols = jnp.dot(occupied.T, col_hot)
    return (pick_rows.astype(jnp.bfloat16), pick_cols)


def sparse_product(activations, blocks, pick_rows, pick_cols):
    row_count = activations.shape[0]
    capacity, tile_rows = pick_rows.shape
    tile_cols = pick_cols.shape[1]
    block = blocks.shape[1]
    split_rows = activations.reshape(row_count, tile_rows, block)
    chosen = jnp.einsum(
        "rik,si->srk", split_rows, pick_rows, preferred_element_type=jnp.float32
    ).astype(jnp.bfloat16)
    stacked = blocks.reshape(capacity, block, block)
    products = lax.dot_general(
        chosen, stacked, (((2,), (1,)), ((0,), (0,))), preferred_element_type=jnp.float32
    )
    placed = jnp.einsum("srn,sj->rjn", products, pick_cols, precision=lax.Precision.HIGHEST)
    return placed.reshape(row_count, tile_cols * block)


def per_device(act_rows, gate_up_mask, gate_blocks, up_blocks, down_mask, down_blocks):
    block = gate_blocks.shape[1]
    capacity = gate_blocks.shape[0] // block
    gate_pick_rows, gate_pick_cols = slot_tables(gate_up_mask, capacity)
    down_pick_rows, down_pick_cols = slot_tables(down_mask, capacity)
    row_piece = lax.all_gather(act_rows, "hid", axis=0, tiled=True)
    gate_part = sparse_product(row_piece, gate_blocks, gate_pick_rows, gate_pick_cols)
    up_part = sparse_product(row_piece, up_blocks, gate_pick_rows, gate_pick_cols)
    stacked = jnp.stack([gate_part, up_part])
    halves = lax.psum_scatter(stacked, "wid", scatter_dimension=1, tiled=True)
    hidden_half = (jax.nn.silu(halves[0]) * halves[1]).astype(jnp.bfloat16)
    hidden = lax.all_gather(hidden_half, "wid", axis=0, tiled=True)
    finished = lax.psum_scatter(
        sparse_product(hidden, down_blocks, down_pick_rows, down_pick_cols),
        "hid",
        scatter_dimension=0,
        tiled=True,
    )
    return finished.astype(jnp.bfloat16)


def solution(mesh):
    in_specs = (
        P(("groups", "hid"), "wid"),
        P(("groups", "wid"), "hid"),
        P(("groups", "wid"), "hid"),
        P(("groups", "wid"), "hid"),
        P(("groups", "hid"), "wid"),
        P(("groups", "hid"), "wid"),
    )
    out_specs = P(("groups", "hid"), "wid")
    return jax.shard_map(
        per_device, mesh=mesh, in_specs=in_specs, out_specs=out_specs, check_vma=False
    )
```

profile of v0, /device:TPU:1, one launch (start us, length us, event | category | flops | bytes accessed | tf_op | source)
XLA Modules:
  0.0 162.9 jit_solution(4053731706294410100)
XLA Ops:
  6.5 0.0 reduce-scatter.3.cloned.1.call-start
  6.5 0.8 reshape.177
  7.4 0.7 broadcast_compare_fusion
  8.1 0.3 reduce-window.24
  8.4 0.1 slice.22
  8.5 0.1 slice_reduce_fusion
  8.6 0.1 add_bitcast_fusion
  8.7 0.1 eq.118
  8.8 27.1 %all_gather.6 = bf16[64,4096]{1,0:T(8,128)(2,1)S(1)} all-gather(bf16[8,4096]{1,0:T(8,128)(2,1)} %param.6), channel_id=1, replica_groups=mesh['groups'=2,'hid'=8,'wid'=2] {'hid'}, dimensions={0}, use_global_device_ids=true | all-gather | bytes 589824 | tf_op jit(solution)/shard_map/all_gather | solution.py:49
  35.9 0.1 copy.12
  36.0 0.7 convolution_bitcast_fusion
  36.7 1.4 convolution_convert_fusion
  38.1 4.5 %fusion.9 = f32[128,64,128]{2,1,0:T(8,128)S(1)} fusion(bf16[128,128,128]{2,1,0:T(8,128)(2,1)} %bitcast.49, bf16[128,64,128]{2,0,1:T(8,128)(2,1)S(1)} %convolution_convert_fusion), kind=kOutput, calls=%fused_computation.11 | convolution fusion | flops 268435456 | bytes 10485760 | tf_op jit(solution)/shard_map/dot_general | solution.py:37
  42.6 4.5 %fusion.11 = f32[64,28,128]{2,1,0:T(8,128)S(1)} fusion(f32[128,28,1]{0,1,2:T(8,128)S(1)} %convolution_bitcast_fusion, f32[128,64,128]{2,1,0:T(8,128)S(1)} %fusion.9), kind=kOutput, calls=%fused_computation.14 | convolution fusion | flops 352321536 | bytes 5126144 | tf_op jit(solution)/shard_map/srn,sj->rjn/dot_general | solution.py:40
  47.2 1.1 stack_reshape.6
  48.3 4.5 %fusion.7 = f32[128,64,128]{2,1,0:T(8,128)S(1)} fusion(bf16[128,128,128]{2,1,0:T(8,128)(2,1)} %bitcast.50, bf16[128,64,128]{2,0,1:T(8,128)(2,1)S(1)} %convolution_convert_fusion), kind=kOutput, calls=%fused_computation.9 | convolution fusion | flops 268435456 | bytes 10485760 | tf_op jit(solution)/shard_map/dot_general | solution.py:37
  52.8 0.0 copy-start
  52.8 4.7 %fusion.14 = f32[64,28,128]{2,1,0:T(8,128)S(1)} fusion(f32[128,28,1]{0,1,2:T(8,128)S(1)} %convolution_bitcast_fusion, f32[128,64,128]{2,1,0:T(8,128)S(1)} %fusion.7), kind=kOutput, calls=%fused_computation.15 | convolution fusion | flops 352321536 | bytes 5126144 | tf_op jit(solution)/shard_map/srn,sj->rjn/dot_general | solution.py:40
  57.5 0.0 copy-start.1
  57.5 0.2 stack_reshape.7
  57.7 0.0 copy-done
  57.7 1.4 pad_maximum_fusion
  59.0 0.0 reduce-scatter.3.cloned.1.call-update
  59.1 0.0 reduce-scatter.5.cloned.1.call-start
  59.1 0.0 copy-done.1
  59.1 0.1 reshape.175
  59.2 0.3 reduce-window.16
  59.5 0.1 slice.20
  59.6 0.1 eq.107
  59.7 0.1 slice_reduce_fusion.1
  59.8 0.1 add_bitcast_fusion.1
  59.9 0.7 convolution_bitcast_fusion.1
  60.6 14.9 %reduce-scatter.3.cloned.1.call-done = f32[2,32,3584]{2,1,0:T(8,128)} async-done(((f32[2,64,3584]{2,1,0:T(8,128)}), f32[2,32,3584]{2,1,0:T(8,128)}) %reduce-scatter.3.cloned.1.call-update) | async-done | bytes 917520 | tf_op jit(solution)/shard_map/reduce_scatter | solution.py:53
  75.5 1.3 fusion.21
  76.8 2.1 %all_gather.7 = bf16[64,3584]{1,0:T(8,128)(2,1)S(1)} all-gather(bf16[32,3584]{1,0:T(8,128)(2,1)S(1)} %fusion.21), channel_id=1, replica_groups=mesh['groups'=2,'hid'=8,'wid'=2] {'wid'}, dimensions={0}, use_global_device_ids=true | all-gather | bytes 688128 | tf_op jit(solution)/shard_map/all_gather | solution.py:55
  78.9 0.3 reshape.182
  79.2 1.3 fusion.19
  80.6 4.5 %fusion.6 = f32[128,64,128]{2,1,0:T(8,128)S(1)} fusion(bf16[128,128,128]{2,1,0:T(8,128)(2,1)} %bitcast.51, bf16[128,64,128]{2,0,1:T(8,128)(2,1)S(1)} %fusion.19), kind=kOutput, calls=%fused_computation.7 | convolution fusion | flops 268435456 | bytes 10485760 | tf_op jit(solution)/shard_map/dot_general | solution.py:37
  85.1 4.6 %fusion = f32[32,64,128]{2,0,1:T(8,128)S(1)} fusion(f32[128,32,1]{0,1,2:T(8,128)S(1)} %convolution_bitcast_fusion.1, f32[128,64,128]{2,1,0:T(8,128)S(1)} %fusion.6), kind=kOutput, calls=%fused_computation | convolution fusion | flops 402653184 | bytes 5259264 | tf_op jit(solution)/shard_map/srn,sj->rjn/dot_general | solution.py:40
  89.6 1.6 copy.31
  91.2 0.0 reduce-scatter.5.cloned.1.call-update
  91.3 63.2 %reduce-scatter.5.cloned.1.call-done = f32[8,4096]{1,0:T(8,128)} async-done(((f32[64,4096]{1,0:T(8,128)}), f32[8,4096]{1,0:T(8,128)}) %reduce-scatter.5.cloned.1.call-update) | async-done | bytes 131088 | tf_op jit(solution)/shard_map/reduce_scatter | solution.py:56
  154.5 1.5 convert_element_type.30
  (7 shorter events, 0.1 us)
Async XLA Ops:
  6.5 69.0 %reduce-scatter.3.cloned.1.call-start = ((), (), s32[]{:S(2)}) async-start(), calls=%async_computation.2 | async-start | bytes 2752512 | tf_op jit(solution)/shard_map/reduce_scatter | solution.py:53
  52.8 4.9 %copy-start = (f32[1,64,3584]{2,1,0:T(8,128)S(1)}, f32[1,64,3584]{2,1,0:T(8,128)}, u32[]{:S(2)}) copy-start(f32[1,64,3584]{2,1,0:T(8,128)} %stack_reshape.6) | copy-start | bytes 2752516
  57.5 1.6 %copy-start.1 = (s32[28,32]{1,0:T(8,128)S(1)}, s32[28,32]{1,0:T(8,128)}, u32[]{:S(2)}) copy-start(s32[28,32]{1,0:T(8,128)} %param.10) | copy-start | bytes 10756
  59.1 95.4 %reduce-scatter.5.cloned.1.call-start = ((), (), s32[]{:S(2)}) async-start(), calls=%async_computation.3 | async-start | bytes 1179648 | tf_op jit(solution)/shard_map/reduce_scatter | solution.py:56
Sparse Core Ops, SparseCore 0:
  59.2 16.2 reduce-scatter.2
  91.4 63.0 reduce-scatter.4
where the time goes:
time: 165 us; the launch traced here: 163 us
  waiting for transfers between devices  78.2 us (47%)
  matrix products  31.4 us (19%)
  blocking collectives  29.3 us (18%)
  between operations  13.5 us (8%)
  other arithmetic  5.73 us (3%)
  local copies, waits for them, and re-layouts  4.66 us (3%)
    reduce_scatter x1, waiting for transfers between devices, per_device(): lax.psum_scatter(sparse_product(hidden, down_blocks, down_pick_rows, down...  63.2 us
    all_gather x1, blocking collectives, per_device(): row_piece = lax.all_gather(act_rows, 'hid', axis=0, tiled=True)  27.1 us
    reduce_scatter x1, waiting for transfers between devices, per_device(): halves = lax.psum_scatter(stacked, 'wid', scatter_dimension=1, tiled=True)  14.9 us
    dot_general x3, matrix products, sparse_product(): jnp.einsum('srn,sj->rjn', products, pick_cols, precision=lax.Precision.HI...  13.8 us
    dot_general x3, matrix products, sparse_product(): lax.dot_general(chosen, stacked, (((2,), (1,)), ((0,), (0,))), preferred_...  13.5 us
  transfers between devices with their start and end apart: 2, of which 2 were waited for; matrix products, arithmetic and copies ran while one was open for 1% of the time, Pallas kernels for 0%

commit v1 on v0

v1 whole, which is shorter than its diff:
```python
import functools

import jax
import jax.numpy as jnp
from jax import lax
from jax.experimental import pallas as pl
from jax.experimental.pallas import tpu as pltpu
from jax.sharding import PartitionSpec as P

F32 = jnp.float32
BF16 = jnp.bfloat16
MESH = pl.DeviceIdType.MESH


def iota(shape, dim):
    return lax.broadcasted_iota(jnp.int32, shape, dim)


def dot(a, b):
    return jnp.dot(a, b, preferred_element_type=F32)


def fill_table(mask_ref, table_ref):
    rows, cols = mask_ref.shape
    cap = table_ref.shape[1]
    mask = mask_ref[...].astype(F32)
    mb = mask.astype(BF16)
    lower = (iota((rows, rows), 1) < iota((rows, rows), 0)).astype(F32).astype(BF16)
    upper = (iota((cols, cols), 0) < iota((cols, cols), 1)).astype(F32).astype(BF16)
    upper_wide = (iota((cols, cap), 0) < iota((cols, cap), 1)).astype(F32).astype(BF16)
    same_wide = (iota((cols, cap), 0) == iota((cols, cap), 1)).astype(F32).astype(BF16)
    rank = dot(lower, mb)
    count = dot(jnp.ones((8, rows), BF16), mb).astype(BF16)
    start = dot(count, upper)[0:1]
    start_wide = dot(count, upper_wide)[0:1]
    count_wide = dot(count, same_wide)[0:1]
    in_row = dot(mb, upper)
    row_start = dot(lower, jnp.sum(mask, axis=1, keepdims=True).astype(BF16) * jnp.ones((1, cols), BF16))
    slot = in_row + row_start
    position = jnp.where(mask > 0, rank + start, -1.0)
    packed = slot + float(cap) * (iota((rows, cols), 0).astype(F32) * 2.0 + jnp.where(rank > 0, 1.0, 0.0))
    lane = iota((rows, cap), 1).astype(F32)
    total = jnp.zeros((rows, cap), F32)
    for c in range(cols):
        total += jnp.where(position[:, c : c + 1] == lane, packed[:, c : c + 1], 0.0)
    found = jnp.sum(total, axis=0, keepdims=True).astype(jnp.int32)
    slot_at = found % cap
    rest = found // cap
    table_ref[0:1, :] = slot_at
    table_ref[1:2, :] = rest // 2
    table_ref[2:3, :] = rest % 2
    table_ref[3:4, :] = jnp.maximum(start_wide + count_wide - 1.0, 0.0).astype(jnp.int32)
    table_ref[4:5, :] = jnp.where(count_wide > 0, 1.0, 0.0).astype(jnp.int32)


def entry(table, row, k, size):
    return jnp.clip(table[row, k], 0, size - 1)


def sparse_product(table, x_ref, w_ref, sums_ref, unroll):
    cap, rows, block = sums_ref.shape

    def step(k, total):
        keep = table[2, k].astype(F32)
        total = total * keep + dot(x_ref[entry(table, 1, k, x_ref.shape[0])], w_ref[entry(table, 0, k, cap)])
        sums_ref[k] = total
        return total

    lax.fori_loop(0, cap, step, jnp.zeros((rows, block), F32), unroll=unroll)


def kernel(
    n_hid, act_ref, gu_mask_ref, gate_hbm, up_hbm, down_mask_ref, down_hbm, out_ref,
    gate_w, up_w, down_w, gathered, wide, x, gu_tab_v, down_tab_v, gu_tab, down_tab,
    sums, gate_own, up_own, gate_send, up_send, gate_recv, up_recv, hidden,
    part, y_send, y_recv, z_send, z_recv,
    w_sem, tab_sem, ag_send, ag_recv, fw_send, wid_send, wid_recv, ry_send, ry_recv, rz_send, rz_recv,
):
    ny = 2
    nz = n_hid // ny
    me = lax.axis_index("hid")
    z, y = me // ny, me % ny
    core = lax.axis_index("wid")
    y_peer = z * ny + (1 - y)
    own_rows, width = act_ref.shape
    block = x.shape[2]
    k_blocks = x.shape[0]
    ff_blocks = hidden.shape[0]
    rows = x.shape[1]

    def z_hid(j):
        return lax.rem(z + j, nz) * ny + y

    def from_hid(j):
        return lax.rem(z + nz - j, nz) * ny + y

    loads = [
        pltpu.make_async_copy(src, dst, w_sem.at[i])
        for i, (src, dst) in enumerate(((gate_hbm, gate_w), (up_hbm, up_w), (down_hbm, down_w)))
    ]
    for load in loads:
        load.start()

    barrier = pltpu.get_barrier_semaphore()
    for j in range(1, nz):
        pl.semaphore_signal(barrier, inc=1, device_id={"hid": z_hid(j)}, device_id_type=MESH)
    pl.semaphore_signal(barrier, inc=1, device_id={"hid": y_peer}, device_id_type=MESH)
    pl.semaphore_signal(barrier, inc=1, device_id={"wid": 1 - core}, device_id_type=MESH)

    for b in range(k_blocks):
        wide[b, 0:own_rows, :] = act_ref[:, b * block : (b + 1) * block].astype(F32)
    gathered[me] = wide[:, 0:own_rows, :].reshape(k_blocks * own_rows, block).astype(BF16)

    pl.semaphore_wait(barrier, nz + 1)

    def send_act(slot, target, send_sem):
        return pltpu.make_async_remote_copy(
            src_ref=gathered.at[slot], dst_ref=gathered.at[slot], send_sem=send_sem,
            recv_sem=ag_recv.at[slot], device_id={"hid": target}, device_id_type=MESH)

    sends = []
    copy = send_act(me, y_peer, fw_send.at[0])
    copy.start()
    sends.append(copy)
    for j in range(1, nz):
        copy = send_act(me, z_hid(j), ag_send.at[j])
        copy.start()
        sends.append(copy)

    fill_table(gu_mask_ref, gu_tab_v)
    gu_copy = pltpu.make_async_copy(gu_tab_v, gu_tab, tab_sem.at[0])
    gu_copy.start()

    for j in range(1, nz):
        slot = from_hid(j)
        send_act(slot, y_peer, fw_send.at[j]).wait_recv()
        copy = send_act(slot, y_peer, fw_send.at[j])
        copy.start()
        sends.append(copy)

    fill_table(down_mask_ref, down_tab_v)
    down_copy = pltpu.make_async_copy(down_tab_v, down_tab, tab_sem.at[1])
    down_copy.start()

    for j in range(nz):
        slot = lax.rem(z + nz - j, nz) * ny + (1 - y)
        send_act(slot, y_peer, fw_send.at[j]).wait_recv()
    for p in range(n_hid):
        wide[:, p * own_rows : (p + 1) * own_rows, :] = (
            gathered[p].astype(F32).reshape(k_blocks, own_rows, block))
    x[...] = wide[...].astype(BF16)

    gu_copy.wait()

    def to_wid(src, dst, i):
        return pltpu.make_async_remote_copy(
            src_ref=src, dst_ref=dst, send_sem=wid_send.at[i], recv_sem=wid_recv.at[i],
            device_id={"wid": 1 - core}, device_id_type=MESH)

    def half(load, w, own, send, recv, i):
        load.wait()
        sparse_product(gu_tab, x, w, sums, 8)

        def column(c, _):
            value = sums[entry(gu_tab, 3, c, sums.shape[0])] * gu_tab[4, c].astype(F32)
            own[c] = value
            send[c] = value.astype(BF16)
            return 0

        lax.fori_loop(0, ff_blocks, column, 0)
        copy = to_wid(send, recv, i)
        copy.start()
        return copy

    gate_copy = half(loads[0], gate_w, gate_own, gate_send, gate_recv, 0)
    up_copy = half(loads[1], up_w, up_own, up_send, up_recv, 1)
    gate_copy.wait_recv()
    up_copy.wait_recv()

    def activate(c, _):
        gate = gate_own[c] + gate_recv[c].astype(F32)
        up = up_own[c] + up_recv[c].astype(F32)
        hidden[c] = (gate / (1.0 + jnp.exp(-gate)) * up).astype(BF16)
        return 0

    lax.fori_loop(0, ff_blocks, activate, 0)

    down_copy.wait()
    loads[2].wait()
    sparse_product(down_tab, hidden, down_w, sums, 8)

    for c in range(k_blocks):
        value = sums[entry(down_tab, 3, c, sums.shape[0])] * down_tab[4, c].astype(F32)
        for p in range(n_hid):
            part[p, c * own_rows : (c + 1) * own_rows, :] = value[p * own_rows : (p + 1) * own_rows]

    def to_y(j):
        return pltpu.make_async_remote_copy(
            src_ref=y_send.at[j], dst_ref=y_recv.at[j], send_sem=ry_send.at[j],
            recv_sem=ry_recv.at[j], device_id={"hid": y_peer}, device_id_type=MESH)

    def to_z(j):
        return pltpu.make_async_remote_copy(
            src_ref=z_send.at[j], dst_ref=z_recv.at[j], send_sem=rz_send.at[j],
            recv_sem=rz_recv.at[j], device_id={"hid": z_hid(j)}, device_id_type=MESH)

    order = list(range(1, nz)) + [0]
    for j in order:
        y_send[j] = part[lax.rem(z + j, nz) * ny + (1 - y)].astype(BF16)
        copy = to_y(j)
        copy.start()
        sends.append(copy)
    for j in range(1, nz):
        to_y(j).wait_recv()
        z_send[j] = (part[z_hid(j)] + y_recv[j].astype(F32)).astype(BF16)
        copy = to_z(j)
        copy.start()
        sends.append(copy)
    to_y(0).wait_recv()
    total = part[me] + y_recv[0].astype(F32)
    for j in range(1, nz):
        to_z(j).wait_recv()
        total += z_recv[j].astype(F32)
    for b in range(k_blocks):
        out_ref[:, b * block : (b + 1) * block] = total[b * own_rows : (b + 1) * own_rows].astype(BF16)

    for copy in sends:
        copy.wait_send()
    gate_copy.wait_send()
    up_copy.wait_send()


def per_device(n_hid, act_rows, gate_up_mask, gate_blocks, up_blocks, down_mask, down_blocks):
    own_rows, width = act_rows.shape
    block = gate_blocks.shape[1]
    cap = gate_blocks.shape[0] // block
    k_blocks, ff_blocks = gate_up_mask.shape
    rows = own_rows * n_hid
    nz = n_hid // 2
    piece = (k_blocks * own_rows, block)
    stacked = (cap, block, block)
    vmem = pl.BlockSpec(memory_space=pltpu.VMEM)
    hbm = pl.BlockSpec(memory_space=pl.ANY)
    dma = pltpu.SemaphoreType.DMA
    return pl.pallas_call(
        functools.partial(kernel, n_hid),
        out_shape=jax.ShapeDtypeStruct(act_rows.shape, BF16),
        in_specs=[vmem, vmem, hbm, hbm, vmem, hbm],
        out_specs=vmem,
        scratch_shapes=[
            pltpu.VMEM(stacked, BF16), pltpu.VMEM(stacked, BF16), pltpu.VMEM(stacked, BF16),
            pltpu.VMEM((n_hid,) + piece, BF16),
            pltpu.VMEM((k_blocks, rows, block), F32),
            pltpu.VMEM((k_blocks, rows, block), BF16),
            pltpu.VMEM((8, cap), jnp.int32), pltpu.VMEM((8, cap), jnp.int32),
            pltpu.SMEM((8, cap), jnp.int32), pltpu.SMEM((8, cap), jnp.int32),
            pltpu.VMEM((cap, rows, block), F32),
            pltpu.VMEM((ff_blocks, rows, block), F32), pltpu.VMEM((ff_blocks, rows, block), F32),
            pltpu.VMEM((ff_blocks, rows, block), BF16), pltpu.VMEM((ff_blocks, rows, block), BF16),
            pltpu.VMEM((ff_blocks, rows, block), BF16), pltpu.VMEM((ff_blocks, rows, block), BF16),
            pltpu.VMEM((ff_blocks, rows, block), BF16),
            pltpu.VMEM((n_hid,) + piece, F32),
            pltpu.VMEM((nz,) + piece, BF16), pltpu.VMEM((nz,) + piece, BF16),
            pltpu.VMEM((nz,) + piece, BF16), pltpu.VMEM((nz,) + piece, BF16),
            dma((3,)), dma((2,)), dma((nz,)), dma((n_hid,)), dma((nz,)),
            dma((2,)), dma((2,)), dma((nz,)), dma((nz,)), dma((nz,)), dma((nz,)),
        ],
        compiler_params=pltpu.CompilerParams(
            collective_id=0, has_side_effects=True, vmem_limit_bytes=60 * 2 ** 20),
        cost_estimate=pl.CostEstimate(
            flops=6 * cap * rows * block * block, bytes_accessed=6 * cap * block * block, transcendentals=0),
    )(
        act_rows, gate_up_mask, gate_blocks.reshape(stacked), up_blocks.reshape(stacked),
        down_mask, down_blocks.reshape(stacked),
    )


def solution(mesh):
    in_specs = (
        P(("groups", "hid"), "wid"),
        P(("groups", "wid"), "hid"),
        P(("groups", "wid"), "hid"),
        P(("groups", "wid"), "hid"),
        P(("groups", "hid"), "wid"),
        P(("groups", "hid"), "wid"),
    )
    out_specs = P(("groups", "hid"), "wid")
    return jax.shard_map(
        functools.partial(per_device, mesh.shape["hid"]),
        mesh=mesh, in_specs=in_specs, out_specs=out_specs, check_vma=False,
    )
```

time: 165 us -> 41.3 us (0.25); the launches traced: 163 us -> 41.1 us
  waiting for transfers between devices: 78.2 us -> 0 us
  Pallas kernels: 0 us -> 39.6 us
  matrix products: 31.4 us -> 0 us
  blocking collectives: 29.3 us -> 0 us
  between operations: 13.5 us -> 0.01 us
  other arithmetic: 5.73 us -> 0 us
  local copies, waits for them, and re-layouts: 4.66 us -> 1.47 us
    reduce_scatter x2 -> x0, waiting for transfers between devices: 78.2 us -> none  [the longest x1 63.2 us: per_device(): lax.psum_scatter(sparse_product(hidden, down_blocks, down_pick_rows, down...]
    pallas_call x0 -> x1, Pallas kernels: none -> 39.6 us  [per_device(): pl.pallas_call(functools.partial(kernel, n_hid), out_shape=jax.ShapeDtype...]
    dot_general x10 -> x0, matrix products: 31.4 us -> none  [the longest x3 13.8 us: sparse_product(): jnp.einsum('srn,sj->rjn', products, pick_cols, precision=lax.Precision.HI...]
    all_gather x2 -> x0, blocking collectives: 29.3 us -> none  [the longest x1 27.1 us: per_device(): row_piece = lax.all_gather(act_rows, 'hid', axis=0, tiled=True)]
    convert_element_type x2 -> x0, other arithmetic: 2.83 us -> none  [the longest x1 1.54 us: per_device(): return finished.astype(jnp.bfloat16)]
    another operation x6 -> x0, local copies, waits for them, and re-layouts: 2.35 us -> none  [the longest x2 1.23 us: per_device(): stacked = jnp.stack([gate_part, up_part])]
    another operation x5 -> x0, other arithmetic: 1.99 us -> none  [the longest x1 1.38 us: per_device(): stacked = jnp.stack([gate_part, up_part])]
  transfers between devices with their start and end apart: 2 -> 0, of which waited for: 2 -> 0; matrix products, arithmetic and copies ran while one was open for 1% -> 0% of each run, Pallas kernels for 0% -> 0%
where the time goes in v1:
time: 41.3 us; the launch traced here: 41.1 us
  Pallas kernels  39.6 us (96%)
  local copies, waits for them, and re-layouts  1.47 us (4%)
    pallas_call x1, Pallas kernels, per_device(): pl.pallas_call(functools.partial(kernel, n_hid), out_shape=jax.ShapeDtype...  39.6 us
    unnamed x1, local copies, waits for them, and re-layouts  1.47 us

profile of v1, /device:TPU:1, one launch (start us, length us, event | category | flops | bytes accessed | tf_op | source)
XLA Modules:
  0.0 41.1 jit_solution(6483200568994528682)
XLA Ops:
  0.0 39.6 %shard_map.64 = bf16[8,4096]{1,0:T(8,128)(2,1)} custom-call(bf16[8,4096]{1,0:T(8,128)(2,1)} %act_ref.1, s32[32,28]{1,0:T(8,128)} %gu_mask_ref.1, bf16[128,128,128]{2,1,0:T(8,128)(2,1)} %bitcast.3, bf16[128,128,128]{2,1,0:T(8,128)(2,1)} %bitcast.4, s32[28,32]{1,0:T(8,128)} %down_mask_ref.1, bf16[128,128,128]{2,1,0:T(8,128)(2,1)} %bitcast.5), custom_call_target="tpu_custom_call" | custom-call | flops 805306368 | bytes 12582912 | tf_op jit(solution)/shard_map/pallas_call | solution.py:245
  39.6 1.5 %copy.8 = bf16[8,4096]{1,0:T(8,128)(2,1)} copy(bf16[8,4096]{1,0:T(8,128)(2,1)} %shard_map.64) | data formatting | bytes 131072

commit v2 on v1

--- a/solution.py
+++ b/solution.py
@@ -159,7 +159,7 @@
 
     def half(load, w, own, send, recv, i):
         load.wait()
-        sparse_product(gu_tab, x, w, sums, 8)
+        sparse_product(gu_tab, x, w, sums, 128)
 
         def column(c, _):
             value = sums[entry(gu_tab, 3, c, sums.shape[0])] * gu_tab[4, c].astype(F32)
@@ -167,7 +167,8 @@
             send[c] = value.astype(BF16)
             return 0
 
-        lax.fori_loop(0, ff_blocks, column, 0)
+        for c in range(ff_blocks):
+            column(c, 0)
         copy = to_wid(send, recv, i)
         copy.start()
         return copy
@@ -183,11 +184,12 @@
         hidden[c] = (gate / (1.0 + jnp.exp(-gate)) * up).astype(BF16)
         return 0
 
-    lax.fori_loop(0, ff_blocks, activate, 0)
+    for c in range(ff_blocks):
+        activate(c, 0)
 
     down_copy.wait()
     loads[2].wait()
-    sparse_product(down_tab, hidden, down_w, sums, 8)
+    sparse_product(down_tab, hidden, down_w, sums, 128)
 
     for c in range(k_blocks):
         value = sums[entry(down_tab, 3, c, sums.shape[0])] * down_tab[4, c].astype(F32)

time: 41.3 us -> 34.3 us (0.83)
  Pallas kernels: 39.6 us -> 32.6 us
    pallas_call x1, Pallas kernels: 39.6 us -> 32.6 us  [per_device(): pl.pallas_call(functools.partial(kernel, n_hid), out_shape=jax.ShapeDtype...]
where the time goes in v2:
time: 34.3 us; the launch traced here: 34.1 us
  Pallas kernels  32.6 us (95%)
  local copies, waits for them, and re-layouts  1.47 us (4%)
    pallas_call x1, Pallas kernels, per_device(): pl.pallas_call(functools.partial(kernel, n_hid), out_shape=jax.ShapeDtype...  32.6 us
    unnamed x1, local copies, waits for them, and re-layouts  1.47 us

profile of v2, /device:TPU:1, one launch (start us, length us, event | category | flops | bytes accessed | tf_op | source)
XLA Modules:
  0.0 34.1 jit_solution(9597641257666065961)
XLA Ops:
  0.0 32.6 %shard_map.64 = bf16[8,4096]{1,0:T(8,128)(2,1)} custom-call(bf16[8,4096]{1,0:T(8,128)(2,1)} %act_ref.1, s32[32,28]{1,0:T(8,128)} %gu_mask_ref.1, bf16[128,128,128]{2,1,0:T(8,128)(2,1)} %bitcast.3, bf16[128,128,128]{2,1,0:T(8,128)(2,1)} %bitcast.4, s32[28,32]{1,0:T(8,128)} %down_mask_ref.1, bf16[128,128,128]{2,1,0:T(8,128)(2,1)} %bitcast.5), custom_call_target="tpu_custom_call" | custom-call | flops 805306368 | bytes 12582912 | tf_op jit(solution)/shard_map/pallas_call | solution.py:247
  32.7 1.5 %copy.8 = bf16[8,4096]{1,0:T(8,128)(2,1)} copy(bf16[8,4096]{1,0:T(8,128)(2,1)} %shard_map.64) | data formatting | bytes 131072

commit v3 on v2

--- a/solution.py
+++ b/solution.py
@@ -70,7 +70,8 @@
 
 
 def kernel(
-    n_hid, act_ref, gu_mask_ref, gate_hbm, up_hbm, down_mask_ref, down_hbm, out_ref,
+    n_hid, act_hbm, gu_mask_hbm, gate_hbm, up_hbm, down_mask_hbm, down_hbm, out_ref,
+    act_ref, gu_mask_ref, down_mask_ref, small_sem,
     gate_w, up_w, down_w, gathered, wide, x, gu_tab_v, down_tab_v, gu_tab, down_tab,
     sums, gate_own, up_own, gate_send, up_send, gate_recv, up_recv, hidden,
     part, y_send, y_recv, z_send, z_recv,
@@ -94,6 +95,13 @@
     def from_hid(j):
         return lax.rem(z + nz - j, nz) * ny + y
 
+    small = [
+        pltpu.make_async_copy(src, dst, small_sem.at[i])
+        for i, (src, dst) in enumerate(
+            ((act_hbm, act_ref), (gu_mask_hbm, gu_mask_ref), (down_mask_hbm, down_mask_ref)))
+    ]
+    for load in small:
+        load.start()
     loads = [
         pltpu.make_async_copy(src, dst, w_sem.at[i])
         for i, (src, dst) in enumerate(((gate_hbm, gate_w), (up_hbm, up_w), (down_hbm, down_w)))
@@ -107,6 +115,7 @@
     pl.semaphore_signal(barrier, inc=1, device_id={"hid": y_peer}, device_id_type=MESH)
     pl.semaphore_signal(barrier, inc=1, device_id={"wid": 1 - core}, device_id_type=MESH)
 
+    small[0].wait()
     for b in range(k_blocks):
         wide[b, 0:own_rows, :] = act_ref[:, b * block : (b + 1) * block].astype(F32)
     gathered[me] = wide[:, 0:own_rows, :].reshape(k_blocks * own_rows, block).astype(BF16)
@@ -127,6 +136,7 @@
         copy.start()
         sends.append(copy)
 
+    small[1].wait()
     fill_table(gu_mask_ref, gu_tab_v)
     gu_copy = pltpu.make_async_copy(gu_tab_v, gu_tab, tab_sem.at[0])
     gu_copy.start()
@@ -138,6 +148,7 @@
         copy.start()
         sends.append(copy)
 
+    small[2].wait()
     fill_table(down_mask_ref, down_tab_v)
     down_copy = pltpu.make_async_copy(down_tab_v, down_tab, tab_sem.at[1])
     down_copy.start()
@@ -247,9 +258,11 @@
     return pl.pallas_call(
         functools.partial(kernel, n_hid),
         out_shape=jax.ShapeDtypeStruct(act_rows.shape, BF16),
-        in_specs=[vmem, vmem, hbm, hbm, vmem, hbm],
+        in_specs=[hbm, hbm, hbm, hbm, hbm, hbm],
         out_specs=vmem,
         scratch_shapes=[
+            pltpu.VMEM(act_rows.shape, BF16), pltpu.VMEM(gate_up_mask.shape, jnp.int32),
+            pltpu.VMEM(down_mask.shape, jnp.int32), dma((3,)),
             pltpu.VMEM(stacked, BF16), pltpu.VMEM(stacked, BF16), pltpu.VMEM(stacked, BF16),
             pltpu.VMEM((n_hid,) + piece, BF16),
             pltpu.VMEM((k_blocks, rows, block), F32),

time: 34.3 us -> 33.4 us (0.974)
  Pallas kernels: 32.6 us -> 31.8 us
    pallas_call x1, Pallas kernels: 32.6 us -> 31.8 us  [per_device(): pl.pallas_call(functools.partial(kernel, n_hid), out_shape=jax.ShapeDtype...]
where the time goes in v3:
time: 33.4 us; the launch traced here: 33.3 us
  Pallas kernels  31.8 us (95%)
  local copies, waits for them, and re-layouts  1.47 us (4%)
    pallas_call x1, Pallas kernels, per_device(): pl.pallas_call(functools.partial(kernel, n_hid), out_shape=jax.ShapeDtype...  31.8 us
    unnamed x1, local copies, waits for them, and re-layouts  1.47 us

profile of v3, /device:TPU:1, one launch (start us, length us, event | category | flops | bytes accessed | tf_op | source)
XLA Modules:
  0.0 33.3 jit_solution(2491368553795211854)
XLA Ops:
  0.0 31.8 %shard_map.64 = bf16[8,4096]{1,0:T(8,128)(2,1)} custom-call(bf16[8,4096]{1,0:T(8,128)(2,1)} %act_hbm.1, s32[32,28]{1,0:T(8,128)} %gu_mask_hbm.1, bf16[128,128,128]{2,1,0:T(8,128)(2,1)} %bitcast.3, bf16[128,128,128]{2,1,0:T(8,128)(2,1)} %bitcast.4, s32[28,32]{1,0:T(8,128)} %down_mask_hbm.1, bf16[128,128,128]{2,1,0:T(8,128)(2,1)} %bitcast.5), custom_call_target="tpu_custom_call" | custom-call | flops 805306368 | bytes 12582912 | tf_op jit(solution)/shard_map/pallas_call | solution.py:258
  31.8 1.5 %copy.8 = bf16[8,4096]{1,0:T(8,128)(2,1)} copy(bf16[8,4096]{1,0:T(8,128)(2,1)} %shard_map.64) | data formatting | bytes 131072
